TPU v7x, 256 devices: a whole 4x4x8 slice. The times are simulated.
256 devices in a mesh: cluster: 32 (over y, z), sub: 8 (over x, core).
Axes of the slice: x: 4, y: 4, z: 8, core: 2. Of those that a mesh axis runs over, the one named last changes fastest.
Arguments:
- right_side: float32 [8, 32, 16, 384], P('sub', 'cluster'), may hold values from -12 to 12
- schur: float32 [8, 32, 768, 768], P('sub', 'cluster'), as said below
- rigid_modes: float32 [8, 32, 6, 768], P('sub', 'cluster'), may hold values from -0.21875 to 0.21875
- mode_count: int32 [8, 32], P('sub', 'cluster'), may hold values from 3 to 6
- face_order: int32 [8, 32, 384], P('sub', 'cluster'), may hold values from 0 to 383, each once within a row
- dual_scale: float32 [8, 32, 384], P('sub', 'cluster'), may hold values from 0.5 to 2
- rigid_loads: float32 [8, 32, 6, 16], P('sub', 'cluster'), may hold values from -6 to 6
- coarse_inverse: float32 [1536, 1536], P(('cluster', 'sub')), as said below
Outputs:
- multipliers: float32 [8, 32, 16, 384], P('sub', 'cluster')
- residual: float32 [8, 32, 16, 384], P('sub', 'cluster')
Inputs may be any that keep to these rules, and one draw needn't show every extreme that they name: rigid-body modes m with m >= mode_count are unused. `face_order`: each subdomain's entries form a permutation of the face unknowns; those of the first subdomain of a chain are unused. `schur`: each subdomain's matrix is symmetric. `coarse_inverse`: symmetric.
All inputs are finite; a program needn't handle non-finite values.
Results may differ from a plain program's by a relative error of at most 0.0003.
Values sent between devices are 32-bit elements; how exact they have to be, the bound alone decides.
A program may use at most 64 MiB of HBM per device.

v0:
```python
import functools

import jax
import jax.numpy as jnp
from jax import lax
from jax.experimental import pallas as pl
from jax.experimental.pallas import tpu as pltpu
from jax.sharding import PartitionSpec as P

MESH = pl.DeviceIdType.MESH
CHAIN = 32
NSUB = 8
NZ = 8
NY = 4
CASES = 16
M = 384
MODES = 6
F32 = jnp.float32
BF16 = jnp.bfloat16
NN = (((1,), (0,)), ((), ()))
NT = (((1,), (1,)), ((), ()))


def parts(v):
    high = v.astype(BF16)
    return high, (v - high.astype(F32)).astype(BF16)


def mul(a, b, dims=NN):
    return lax.dot_general(a, b, dims, preferred_element_type=F32)


def mul3(a, b, dims=NN):
    ah, al = parts(a)
    bh, bl = parts(b)
    n = a.shape[0]
    both = mul(jnp.concatenate([ah, al], axis=0), bh, dims)
    return both[:n] + both[n:] + mul(ah, bl, dims)


def mulw(a, wh, wl):
    ah, al = parts(a)
    n = a.shape[0]
    both = mul(jnp.concatenate([ah, al], axis=0), wh)
    return both[:n] + both[n:] + mul(ah, wl)


def iota(shape, dim):
    return lax.broadcasted_iota(jnp.int32, shape, dim)


def fold_lanes(v):
    v = v + pltpu.roll(v, 64, 1)
    v = v + pltpu.roll(v, 32, 1)
    return v + pltpu.roll(v, 16, 1)


def inverse_of(matrix):
    lane = iota((CASES, 128), 1)
    row = iota((CASES, 128), 0)
    left = lane < CASES
    tile = jnp.where(left, matrix, jnp.where(lane == row + CASES, 1.0, 0.0))
    for k in range(CASES):
        column = jnp.broadcast_to(tile[:, k : k + 1], (CASES, 128))
        pivot_row = jnp.broadcast_to(tile[k : k + 1, :], (CASES, 128))
        pivot = jnp.broadcast_to(tile[k : k + 1, k : k + 1], (CASES, 128))
        scaled = pivot_row / pivot
        tile = jnp.where(row == k, scaled, tile - column * scaled)
    return tile[:, CASES : 2 * CASES]


def exact(a, b, dims=NN):
    return lax.dot_general(
        a, b, dims, precision=lax.Precision.HIGHEST, preferred_element_type=F32
    )


def kernel(
    right_ref, schur_hbm, modes_ref, count_ref, order_ref, scale_ref, loads_ref, coarse_ref,
    mult_ref, resid_ref,
    schur_ref, sh_ref, sl_ref, wh_ref, wl_ref, xa_ref,
    crow_ref, ch_ref, cl_ref,
    small1, small1_in, small2, small2_in,
    large1, large1_in, large2, large2_in,
    modes_out, modes_in,
    wide_fwd, wide_fwd_in, wide_back, wide_back_in,
    fwd, fwd_in, back, back_in,
    tmp_ref,
    load_sem, coarse_ssem, coarse_rsem, send1, recv1, send2, recv2, nb_ssem, nb_rsem,
):
    j = lax.axis_index("cluster")
    s = lax.axis_index("sub")
    y = j // NZ
    z = j % NZ
    me2 = y * NSUB + s

    load = pltpu.make_async_copy(schur_hbm, schur_ref, load_sem)
    load.start()

    def chain(d):
        return ((j + d + CHAIN) % CHAIN, s)

    def zpeer(i):
        return (y * NZ + (z + i) % NZ, s)

    def peer2(dy, ds):
        return (((y + dy) % NY) * NZ + z, (s + ds) % NSUB)

    def each_peer2(act):
        for dy in (2, 1, 3):
            def body(i, c, dy=dy):
                act(dy, i + 4)
                return c

            lax.fori_loop(0, NSUB, body, 0)
        for ds in (4, 3, 5, 2, 6, 1, 7):
            act(0, ds)

    def each_z(act):
        for i in (4, 3, 5, 2, 6, 1, 7):
            act(i)

    barrier = pltpu.get_barrier_semaphore()

    def greet(device):
        pl.semaphore_signal(barrier, inc=1, device_id=device, device_id_type=MESH)

    each_peer2(lambda dy, ds: greet(peer2(dy, ds)))
    each_z(lambda i: greet(zpeer(i)))
    for d in (-2, -1, 1, 2):
        greet(chain(d))

    count = count_ref[...]
    active = jnp.where(iota((MODES, 1), 0) < count, 1.0, 0.0)
    basis = modes_ref[...] * active
    lane = iota((8, 128), 1)
    sub8 = iota((8, 128), 0)
    tmp_ref[...] = jnp.zeros((8, 128), F32)
    tmp_ref[0:MODES, 0:CASES] = loads_ref[...] * active
    spread = fold_lanes(tmp_ref[...])
    own_loads = jnp.sum(jnp.where(lane // CASES == sub8, spread, 0.0), axis=0, keepdims=True)
    small1[0] = jnp.concatenate([own_loads, jnp.zeros((1, 128), F32)], axis=0)

    hot = jnp.where(iota((M, M), 0) == order_ref[...], 1.0, 0.0).astype(BF16)
    bh, bl = parts(basis[:, :M])
    third = (basis[:, :M] - bh.astype(F32) - bl.astype(F32)).astype(BF16)
    permuted = -(mul(bh, hot, NT) + mul(bl, hot, NT) + mul(third, hot, NT))
    modes_out[...] = jnp.zeros((8, M), F32)
    modes_out[0:MODES, :] = permuted

    pl.semaphore_wait(barrier, 31 + 7 + 4)

    def neighbour(k, src, dst, d):
        return pltpu.make_async_remote_copy(
            src_ref=src, dst_ref=dst, send_sem=nb_ssem.at[k], recv_sem=nb_rsem.at[k],
            device_id=chain(d), device_id_type=MESH,
        )

    def send_stage1(r, src, dst):
        def one(i):
            pltpu.make_async_remote_copy(
                src_ref=src, dst_ref=dst.at[z], send_sem=send1.at[r], recv_sem=recv1.at[r],
                device_id=zpeer(i), device_id_type=MESH,
            ).start()

        each_z(one)
        dst[z] = src[...]

    def wait_stage1(r, dst):
        w = dst.at[pl.ds(0, NZ - 1)]
        pltpu.make_async_copy(w, w, recv1.at[r]).wait()

    def send_stage2(r, src, dst):
        def one(dy, ds):
            pltpu.make_async_remote_copy(
                src_ref=src, dst_ref=dst.at[me2], send_sem=send2.at[r], recv_sem=recv2.at[r],
                device_id=peer2(dy, ds), device_id_type=MESH,
            ).start()

        each_peer2(one)
        dst[me2] = src[...]

    def wait_stage2(r, dst):
        w = dst.at[pl.ds(0, NY * NSUB - 1)]
        pltpu.make_async_copy(w, w, recv2.at[r]).wait()

    send_stage1(0, small1.at[0], small1_in.at[0])

    modes_copy = neighbour(0, modes_out, modes_in, -1)
    modes_copy.start()
    colour = j % 4
    coarse_copies = []
    for k, d in enumerate((1, -1, -2)):
        coarse_copies.append(
            pltpu.make_async_remote_copy(
                src_ref=coarse_ref, dst_ref=crow_ref.at[colour], send_sem=coarse_ssem.at[k],
                recv_sem=coarse_rsem.at[k], device_id=chain(d), device_id_type=MESH,
            )
        )
        coarse_copies[-1].start()
    crow_ref[colour] = coarse_ref[...]

    load.wait()

    def split_rows(i, c):
        rows = pl.ds(pl.multiple_of(i * 128, 128), 128)
        high, low = parts(schur_ref[rows, :])
        sh_ref[rows, :] = high
        sl_ref[rows, :] = low
        for ref, part in ((sh_ref, high), (sl_ref, low)):
            ref[rows, 0:M] = (-mul(part[:, :M], hot, NT)).astype(BF16)
        return c

    lax.fori_loop(0, 6, split_rows, 0)

    def split_columns(i, c):
        cols = pl.ds(pl.multiple_of(i * 128, 128), 128)
        for ref in (sh_ref, sl_ref):
            ref[0:M, cols] = (-mul(hot, ref[0:M, cols])).astype(BF16)
        return c

    lax.fori_loop(0, 6, split_columns, 0)

    first = j > 0
    last = j < CHAIN - 1

    def apply_send(k, rows, out, out_in):
        out[...] = rows
        copy = neighbour(k, out, out_in, 1)
        copy.start()
        return copy

    def apply_middle(copy, k, rows, out_in, ret, ret_in):
        copy.wait_recv()
        before = jnp.where(first, out_in[...], 0.0)
        image = mulw(jnp.concatenate([before, rows], axis=1), sh_ref[...], sl_ref[...])
        ret[...] = image[:, :M]
        copy_back = neighbour(k, ret, ret_in, -1)
        copy_back.start()
        return copy_back, image[:, M:]

    def apply_end(copy_back, own, ret_in):
        copy_back.wait_recv()
        return own + jnp.where(last, ret_in[...], 0.0)

    modes_copy.wait_recv()
    following = jnp.where(last, modes_in[...], 0.0)
    tmp_modes = jnp.concatenate([basis[:, M:], jnp.zeros((2, M), F32)], axis=0)
    xa_ref[:, 0:M] = jnp.zeros((32, M), F32)
    xa_ref[pl.ds(pl.multiple_of(colour * 8, 8), 8), 0:M] = tmp_modes
    xa_ref[pl.ds(pl.multiple_of(((j + 1) % 4) * 8, 8), 8), 0:M] = following
    expand = xa_ref[:, 0:M]
    wide_copy = apply_send(1, expand, wide_fwd, wide_fwd_in)

    pieces = []
    for block in (tmp_modes, following):
        for m in range(MODES):
            pieces.append(jnp.broadcast_to(block[m : m + 1, :], (CASES, M)))
        pieces.append(jnp.zeros((32, M), F32))
    weights = jnp.transpose(jnp.concatenate(pieces, axis=0))
    wh, wl = parts(weights)
    wh_ref[...] = wh
    wl_ref[...] = wl

    wide_back_copy, wide_own = apply_middle(wide_copy, 2, expand, wide_fwd_in, wide_back, wide_back_in)

    own_case = (iota((CASES, 256), 1) % CASES) == iota((CASES, 256), 0)
    below = sub8 > 0

    def coefficients(field):
        product = mulw(field, wh_ref[...], wl_ref[...])
        flat = jnp.sum(jnp.where(own_case, product, 0.0), axis=0, keepdims=True)
        return flat[:, :128], flat[:, 128:]

    def combine(own, nxt):
        moved = jnp.where(below, pltpu.roll(nxt, 1, 0), 0.0)
        end = jnp.broadcast_to(nxt[NZ - 1 : NZ, :], (8, 128))
        rest = jnp.where(
            sub8 == 0,
            pltpu.roll(end, 96, 1),
            jnp.where(sub8 == 1, pltpu.roll(end, 64, 1), pltpu.roll(end, 32, 1)),
        )
        return own + moved + jnp.where((lane >= 96) & (sub8 < 3), rest, 0.0)

    def stage2_small(r):
        wait_stage1(r, small1_in.at[r])
        got = small1_in[r]
        small2[r] = combine(got[:, 0, :], got[:, 1, :])
        send_stage2(r, small2.at[r], small2_in.at[r])

    slot = iota((8, 8, 128), 2) // CASES == iota((8, 8, 128), 0)

    def coarse(values):
        gh, gl = parts(values)
        both = mul(ch_ref[...], jnp.concatenate([gh, gl], axis=1))
        full = both[:, :128] + both[:, 128:] + mul(cl_ref[...], gh)
        picked = [
            jnp.sum(jnp.where(slot, full[c * 64 : (c + 1) * 64].reshape(8, 8, 128), 0.0), axis=0)
            for c in range(4)
        ]
        turned = jnp.transpose(jnp.concatenate(picked, axis=0))
        return jnp.sum(turned.reshape(8, CASES, 32), axis=0)

    def gram_rows(a, blocks):
        rep = jnp.concatenate([b for b in blocks for _ in range(8)], axis=0)
        product = mul3(a, rep, NT)
        rows = []
        for k in range(len(blocks)):
            tile = product[:, k * 128 : (k + 1) * 128].reshape(2, 8, 128)
            keep = iota((2, 8, 128), 2) // CASES == iota((2, 8, 128), 1)
            rows.append(jnp.sum(jnp.where(keep, tile, 0.0), axis=1))
        return rows

    def gram_matrix(pair):
        wide = jnp.broadcast_to(pair[:, None, :], (2, 8, 128))
        keep = iota((2, 8, 128), 2) // CASES == iota((2, 8, 128), 1)
        return fold_lanes(jnp.where(keep, wide, 0.0).reshape(CASES, 128))

    def send_large(r, own, nxt, rows):
        pad = jnp.zeros((8 - 2 - 2 * len(rows), 128), F32)
        large1[r] = jnp.concatenate([own, nxt, *rows, pad], axis=0)
        send_stage1(3 + r, large1.at[r], large1_in.at[r])

    def stage2_large(r):
        wait_stage1(3 + r, large1_in.at[r])
        got = large1_in[r]
        large2[r] = jnp.concatenate(
            [combine(got[:, 0, :], got[:, 1, :]), jnp.sum(got, axis=0)], axis=0
        )
        send_stage2(3 + r, large2.at[r], large2_in.at[r])

    def finish_large(r):
        wait_stage2(3 + r, large2_in.at[r])
        got = large2_in[r]
        sums = jnp.sum(got[:, 8:, :], axis=0)
        return got[:, :8, :].reshape(256, 128), sums

    def finish_small(r):
        wait_stage2(r, small2_in.at[r])
        return small2_in[r].reshape(256, 128)

    stage2_small(0)

    for copy in coarse_copies:
        copy.wait_recv()
    ch, cl = parts(crow_ref[...].reshape(256, 256))
    ch_ref[...] = ch
    cl_ref[...] = cl
    xa_ref[:, M:] = apply_end(wide_back_copy, wide_own, wide_back_in)

    right = right_ref[...]
    scale = scale_ref[...]
    y0 = coarse(finish_small(0))
    moved = mul3(y0, xa_ref[...])
    mult = moved[:, :M]
    tt = right - moved[:, M:]

    own, nxt = coefficients(tt)
    small1[1] = jnp.concatenate([own, nxt], axis=0)
    send_stage1(1, small1.at[1], small1_in.at[1])
    stage2_small(1)
    y1 = coarse(finish_small(1))
    resid = tt - mul3(y1, xa_ref[:, 0:M])
    scaled = scale * resid

    own, nxt = coefficients(scaled)
    small1[2] = jnp.concatenate([own, nxt], axis=0)
    send_stage1(2, small1.at[2], small1_in.at[2])
    copy = apply_send(3, scaled, fwd.at[0], fwd_in.at[0])
    copy_back, image_own = apply_middle(copy, 4, scaled, fwd_in.at[0], back.at[0], back_in.at[0])
    stage2_small(2)
    image = apply_end(copy_back, image_own, back_in.at[0])
    y2 = coarse(finish_small(2))
    moved = mul3(y2, xa_ref[...])
    direction = scaled - moved[:, :M]
    image = image - moved[:, M:]

    own, nxt = coefficients(image)
    send_large(0, own, nxt, gram_rows(direction, (image, resid)))
    stage2_large(0)
    values, sums = finish_large(0)
    y3 = coarse(values)
    projected = image - mul3(y3, xa_ref[:, 0:M])
    curvature_inverse = inverse_of(gram_matrix(sums[2:4]))
    descent = gram_matrix(sums[4:6])
    step = exact(curvature_inverse, descent)
    step_t = jnp.transpose(step)[0:CASES, :]
    mult = mult + exact(step_t, direction)
    resid = resid - exact(step_t, projected)
    scaled = scale * resid

    own, nxt = coefficients(scaled)
    send_large(1, own, nxt, gram_rows(projected, (scaled,)))
    copy = apply_send(5, scaled, fwd.at[1], fwd_in.at[1])
    copy_back, image_own = apply_middle(copy, 6, scaled, fwd_in.at[1], back.at[1], back_in.at[1])
    stage2_large(1)
    next_image = apply_end(copy_back, image_own, back_in.at[1])
    values, sums = finish_large(1)
    y4 = coarse(values)
    moved = mul3(y4, xa_ref[...])
    correction = -exact(curvature_inverse, gram_matrix(sums[2:4]))
    correction_t = jnp.transpose(correction)[0:CASES, :]
    mixed = exact(correction_t, jnp.concatenate([direction, image], axis=1))
    direction = scaled - moved[:, :M] + mixed[:, :M]
    image = next_image - moved[:, M:] + mixed[:, M:]

    own, nxt = coefficients(image)
    send_large(2, own, nxt, gram_rows(direction, (image, resid)))
    stage2_large(2)
    values, sums = finish_large(2)
    y5 = coarse(values)
    projected = image - mul3(y5, xa_ref[:, 0:M])
    step = exact(inverse_of(gram_matrix(sums[2:4])), gram_matrix(sums[4:6]))
    step_t = jnp.transpose(step)[0:CASES, :]
    mult_ref[...] = mult + exact(step_t, direction)
    resid_ref[...] = resid - exact(step_t, projected)

    modes_copy.wait_send()
    for c in coarse_copies:
        c.wait_send()
    for k, src, d in (
        (1, wide_fwd, 1), (2, wide_back, -1), (3, fwd.at[0], 1), (4, back.at[0], -1),
        (5, fwd.at[1], 1), (6, back.at[1], -1),
    ):
        pltpu.make_async_copy(src, src, nb_ssem.at[k]).wait()
    for r in range(6):
        in1 = small1_in.at[r] if r < 3 else large1_in.at[r - 3]
        in2 = small2_in.at[r] if r < 3 else large2_in.at[r - 3]
        w = in1.at[pl.ds(0, NZ - 1)]
        pltpu.make_async_copy(w, w, send1.at[r]).wait()
        w = in2.at[pl.ds(0, NY * NSUB - 1)]
        pltpu.make_async_copy(w, w, send2.at[r]).wait()


def coarse_blocks(rows):
    c = rows.reshape(MODES, NY, NZ, NSUB, MODES)
    main = jnp.transpose(c, (4, 0, 1, 3, 2))
    spare = c[:, 1:, 0].reshape(MODES, NY - 1, NSUB, 3, 2)
    spare = jnp.transpose(spare, (4, 0, 1, 2, 3))
    spare = jnp.pad(spare, ((0, 0), (0, 0), (0, 1), (0, 0), (0, NZ - 3)))
    both = jnp.concatenate([main, spare], axis=0)
    both = jnp.pad(both, ((0, 0), (0, 2), (0, 0), (0, 0), (0, 0)))
    return both.reshape(64, 256)


def shards(right, schur, modes, count, order, scale, loads, coarse):
    vmem = pl.BlockSpec(memory_space=pltpu.VMEM)
    dma = pltpu.SemaphoreType.DMA
    v = pltpu.VMEM
    mult, resid = pl.pallas_call(
        kernel,
        name="feti",
        out_shape=(jax.ShapeDtypeStruct((CASES, M), F32),) * 2,
        in_specs=[vmem, pl.BlockSpec(memory_space=pl.ANY)] + [vmem] * 6,
        out_specs=(vmem, vmem),
        scratch_shapes=[
            v((768, 768), F32), v((768, 768), BF16), v((768, 768), BF16),
            v((M, 256), BF16), v((M, 256), BF16), v((32, 768), F32),
            v((4, 64, 256), F32), v((256, 256), BF16), v((256, 256), BF16),
            v((3, 2, 128), F32), v((3, NZ, 2, 128), F32),
            v((3, 8, 128), F32), v((3, 32, 8, 128), F32),
            v((3, 8, 128), F32), v((3, NZ, 8, 128), F32),
            v((3, 16, 128), F32), v((3, 32, 16, 128), F32),
            v((8, M), F32), v((8, M), F32),
            v((32, M), F32), v((32, M), F32), v((32, M), F32), v((32, M), F32),
            v((2, 16, M), F32), v((2, 16, M), F32), v((2, 16, M), F32), v((2, 16, M), F32),
            v((8, 128), F32),
            dma, dma((3,)), dma((3,)), dma((6,)), dma((6,)), dma((6,)), dma((6,)),
            dma((7,)), dma((7,)),
        ],
        compiler_params=pltpu.CompilerParams(
            collective_id=0, has_side_effects=True, vmem_limit_bytes=40 * 1024 * 1024
        ),
    )(
        right.reshape(CASES, M), schur.reshape(768, 768), modes.reshape(MODES, 768), count,
        order.reshape(1, M), scale.reshape(1, M), loads.reshape(MODES, CASES),
        coarse_blocks(coarse),
    )
    return mult.reshape(1, 1, CASES, M), resid.reshape(1, 1, CASES, M)


def solution(mesh):
    field = P("sub", "cluster", None, None)
    return jax.shard_map(
        shards,
        mesh=mesh,
        in_specs=(
            field, field, field, P("sub", "cluster"), P("sub", "cluster", None),
            P("sub", "cluster", None), field, P(("cluster", "sub"), None),
        ),
        out_specs=(field, field),
        check_vma=False,
    )
```

profile of v0, /device:TPU:1, one launch (start us, length us, event | category | flops | bytes accessed | tf_op | source)
XLA Modules:
  0.0 91.5 jit_solution(1628483847683108936)
XLA Ops:
  0.6 1.6 %reshape.40 = f32[6,4,8,8,6]{4,3,2,1,0:T(8,128)S(1)} reshape(f32[6,1536]{1,0:T(8,128)} %param.15) | data formatting | bytes 73728 | tf_op jit(solution)/shard_map/reshape | solution.py:436
  2.2 0.2 copy.11
  2.4 0.4 copy.12
  2.8 0.2 select_maximum_fusion
  3.0 0.0 copy-start.4
  3.0 0.0 copy-start.5
  3.0 0.0 copy-start
  3.0 0.0 copy-start.1
  3.0 0.0 copy-start.2
  3.0 0.0 copy-start.3
  3.1 1.5 %copy.16 = f32[8,6,4,8,8]{4,3,2,1,0:T(8,128)} copy(f32[8,6,4,8,8]{0,3,4,2,1:T(8,128)S(1)} %select_maximum_fusion) | data formatting | bytes 98304
  4.5 1.3 %pad.9.clone = f32[8,8,4,8,8]{4,3,2,1,0:T(8,128)S(1)} pad(f32[8,6,4,8,8]{4,3,2,1,0:T(8,128)} %copy.16, f32[]{:T(128)} %constant.2.clone.1), padding=0_0x0_2x0_0x0_0x0_0 | pad | bytes 114692 | tf_op jit(solution)/shard_map/jit(_pad)/pad | solution.py:442
  5.8 0.5 reshape.41.coarse_ref
  6.3 0.0 copy-done.4
  6.3 0.0 copy-done.5
  7.0 0.0 copy-done
  7.0 0.0 copy-done.1
  7.0 0.0 copy-done.2
  7.0 0.0 copy-done.3
  7.0 83.2 %feti.1 = (f32[16,384]{1,0:T(8,128)S(1)}, f32[16,384]{1,0:T(8,128)S(1)}) custom-call(f32[16,384]{1,0:T(8,128)S(1)} %bitcast.20, f32[768,768]{1,0:T(8,128)S(1)} %bitcast.18, f32[6,768]{1,0:T(8,128)S(1)} %bitcast.19, s32[1,1]{1,0:T(1,128)S(6)} %copy.23.count_ref, s32[1,384]{1,0:T(1,128)S(1)} %bitcast.24, f32[1,384]{1,0:T(1,128)S(1)} %bitcast.25, ...), custom_call_target="tpu_custom_call" | custom-call | tf_op jit(solution)/shard_map/feti/pallas_call | solution.py:450
  90.3 0.6 copy.24
  90.9 0.6 copy.25
  (4 shorter events, 0.1 us)
Async XLA Ops:
  3.0 3.3 %copy-start.4 = (f32[1,1,6,768]{3,1,2,0:T(1,128)S(1)}, f32[1,1,6,768]{3,1,2,0:T(1,128)}, u32[]{:S(2)}) copy-start(f32[1,1,6,768]{3,1,2,0:T(1,128)} %param.10) | copy-start | bytes 55300
  3.0 3.3 %copy-start.5 = (f32[1,1,6,16]{3,1,2,0:T(1,128)S(1)}, f32[1,1,6,16]{3,1,2,0:T(1,128)}, u32[]{:S(2)}) copy-start(f32[1,1,6,16]{3,1,2,0:T(1,128)} %param.14) | copy-start | bytes 1156
  3.0 4.0 %copy-start = (f32[1,1,768,768]{3,2,1,0:T(8,128)S(1)}, f32[1,1,768,768]{3,2,1,0:T(8,128)}, u32[]{:S(2)}) copy-start(f32[1,1,768,768]{3,2,1,0:T(8,128)} %param.9) | copy-start | bytes 7077892
  3.0 4.0 %copy-start.1 = (f32[1,1,16,384]{3,2,1,0:T(8,128)S(1)}, f32[1,1,16,384]{3,2,1,0:T(8,128)}, u32[]{:S(2)}) copy-start(f32[1,1,16,384]{3,2,1,0:T(8,128)} %param.8) | copy-start | bytes 73732
  3.0 4.0 %copy-start.2 = (s32[1,1,384]{2,1,0:T(1,128)S(1)}, s32[1,1,384]{2,1,0:T(1,128)}, u32[]{:S(2)}) copy-start(s32[1,1,384]{2,1,0:T(1,128)} %param.12) | copy-start | bytes 4612
  3.0 4.0 %copy-start.3 = (f32[1,1,384]{2,1,0:T(1,128)S(1)}, f32[1,1,384]{2,1,0:T(1,128)}, u32[]{:S(2)}) copy-start(f32[1,1,384]{2,1,0:T(1,128)} %param.13) | copy-start | bytes 4612
where the time goes:
time: 91.7 us; the launch traced here: 91.5 us
  Pallas kernels  83.2 us (91%)
  local copies, waits for them, and re-layouts  6.67 us (7%)
  between operations  1.43 us (2%)
    pallas_call x1, Pallas kernels, shards(): pl.pallas_call(kernel, name='feti', out_shape=(jax.ShapeDtypeStruct((CASE...  83.2 us
    unnamed x17, local copies, waits for them, and re-layouts  2.72 us

commit v1 on v0

v1 whole, which is shorter than its diff:
```python
import functools

import jax
import jax.numpy as jnp
from jax import lax
from jax.experimental import pallas as pl
from jax.experimental.pallas import tpu as pltpu
from jax.sharding import PartitionSpec as P

MESH = pl.DeviceIdType.MESH
CHAIN = 32
NZ = 8
NY = 4
NX = 4
NC = 1536
CASES = 16
M = 384
MODES = 6
F32 = jnp.float32
BF16 = jnp.bfloat16
NN = (((1,), (0,)), ((), ()))
NT = (((1,), (1,)), ((), ()))
TN = (((0,), (0,)), ((), ()))


def parts(v):
    high = v.astype(BF16)
    return high, (v - high.astype(F32)).astype(BF16)


def mul(a, b, dims=NN):
    return lax.dot_general(a, b, dims, preferred_element_type=F32)


def mul3(a, b, dims=NN):
    ah, al = parts(a)
    bh, bl = parts(b)
    n = a.shape[0]
    both = mul(jnp.concatenate([ah, al], axis=0), bh, dims)
    return both[:n] + both[n:] + mul(ah, bl, dims)


def mulw(a, wh, wl):
    ah, al = parts(a)
    n = a.shape[0]
    both = mul(jnp.concatenate([ah, al], axis=0), wh)
    return both[:n] + both[n:] + mul(ah, wl)


def iota(shape, dim):
    return lax.broadcasted_iota(jnp.int32, shape, dim)


def fold_lanes(v):
    v = v + pltpu.roll(v, 64, 1)
    v = v + pltpu.roll(v, 32, 1)
    return v + pltpu.roll(v, 16, 1)


def eliminate(matrix, right):
    shape = (CASES, 2 * CASES)
    row = iota(shape, 0)
    tile = jnp.concatenate([matrix, right], axis=1)
    for k in range(0, CASES, 2):
        c1 = jnp.broadcast_to(tile[:, k : k + 1], shape)
        c2 = jnp.broadcast_to(tile[:, k + 1 : k + 2], shape)
        r1 = jnp.broadcast_to(tile[k : k + 1, :], shape)
        r2 = jnp.broadcast_to(tile[k + 1 : k + 2, :], shape)
        p11 = jnp.broadcast_to(c1[k : k + 1, :], shape)
        p21 = jnp.broadcast_to(c1[k + 1 : k + 2, :], shape)
        p12 = jnp.broadcast_to(c2[k : k + 1, :], shape)
        p22 = jnp.broadcast_to(c2[k + 1 : k + 2, :], shape)
        factor = p21 / p11
        s2 = (r2 - factor * r1) / (p22 - factor * p12)
        s1 = (r1 - p12 * s2) / p11
        rest = tile - c1 * s1 - c2 * s2
        tile = jnp.where(row == k, s1, jnp.where(row == k + 1, s2, rest))
    return tile[:, CASES:]


def exact(a, b, dims=NN):
    return lax.dot_general(
        a, b, dims, precision=lax.Precision.HIGHEST, preferred_element_type=F32
    )


FACES = (
    (2, 2), (2, 1), (2, 3), (1, 2), (3, 2), (2, 0), (0, 2), (1, 1), (1, 3), (3, 1), (3, 3),
    (0, 1), (0, 3), (1, 0), (3, 0), (0, 0),
)


def kernel(
    right_ref, schur_hbm, modes_ref, count_ref, order_ref, scale_ref, loads_ref, coarse_ref,
    mult_ref, resid_ref,
    schur_ref, sh_ref, sl_ref, wh_ref, wl_ref, xa_ref,
    cp_ref, crow_ref, ch_ref, cl_ref,
    out_ref, in_ref, pair_out, pair_in,
    gz_out, gz_in, gy_out, gy_in, gc_out, gc_in,
    left_out, left_in, right_out, right_in,
    fwd, fwd_in, wide_back, wide_back_in, back, back_in,
    tmp_ref,
    load_sem, plane_sem, all_sem, coarse_ssem, coarse_rsem, send, recv, pair_ssem, pair_rsem,
    gz_ssem, gz_rsem, gy_ssem, gy_rsem, gc_ssem, gc_rsem, nb_ssem, nb_rsem,
):
    j = lax.axis_index("cluster")
    s = lax.axis_index("sub")
    y = j // NZ
    z = j % NZ
    x = s // 2
    core = s % 2
    other = s + 1 - 2 * core
    place = j * NX + x
    face = y * NX + x

    load = pltpu.make_async_copy(schur_hbm, schur_ref, load_sem)
    load.start()

    def chain(d):
        return ((j + d + CHAIN) % CHAIN, s)

    def beside(d):
        return ((j + d + CHAIN) % CHAIN, other)

    def peer(dy, dx, dz):
        return (((y + dy) % NY) * NZ + (z + dz) % NZ, ((x + dx) % NX) * 2 + core)

    def z_offset(i):
        half = (i + 1) // 2
        return 4 + half * (1 - 2 * (i % 2))

    def run(faces, low, high, act):
        for dy, dx in faces:
            def body(i, c, dy=dy, dx=dx):
                act(dy, dx, z_offset(i))
                return c

            lax.fori_loop(low, high, body, 0)

    def far_peers(act):
        run(FACES[:11], 0, 5, act)
        run(FACES[:5], 5, 8, act)

    def near_peers(act):
        run(FACES[11:], 0, 5, act)
        run(FACES[5:15], 5, 8, act)
        run(FACES[15:], 5, 7, act)

    def every_peer(act):
        far_peers(act)
        near_peers(act)

    barrier = pltpu.get_barrier_semaphore()

    def greet(device):
        pl.semaphore_signal(barrier, inc=1, device_id=device, device_id_type=MESH)

    for dz in (4, 3, 5, 2, 6, 1, 7):
        greet(peer(0, 0, dz))
    for d in (-2, 2, -1, 1):
        greet(chain(d))
        greet(beside(d))
    for d in (2, 1, 3):
        greet(peer(d, 0, 0))
        greet(peer(0, d, 0))
    greet(beside(0))

    count = count_ref[...]
    active = jnp.where(iota((MODES, 1), 0) < count, 1.0, 0.0)
    basis = modes_ref[:, 0, :] * active
    sub8 = iota((8, 128), 0)
    tmp_ref[...] = jnp.zeros((8, 128), F32)
    tmp_ref[0:MODES, 0:CASES] = loads_ref[:, 0, :] * active
    spread = fold_lanes(tmp_ref[...])
    own_loads = jnp.sum(
        jnp.where(iota((8, 128), 1) // CASES == sub8, spread, 0.0), axis=0, keepdims=True
    )
    out_ref[0] = jnp.concatenate([own_loads, jnp.zeros((1, 128), F32)], axis=0)

    hot = jnp.where(iota((M, M), 0) == order_ref[...], 1.0, 0.0).astype(BF16)
    bh, bl = parts(basis[:, :M])
    permuted = -(mul(bh, hot, NT) + mul(bl, hot, NT))
    left_out[...] = jnp.concatenate([permuted, jnp.zeros((2, M), F32)], axis=0)
    right_out[...] = jnp.concatenate([basis[:, M:], jnp.zeros((2, M), F32)], axis=0)

    wanted = 12 * iota((NC, 128), 1)
    pick = jnp.where(iota((NC, 128), 0) == wanted, 1.0, 0.0).astype(BF16)
    rows = jnp.concatenate([coarse_ref[...], jnp.zeros((2, NC), F32)], axis=0)
    for c in range(2):
        shifted = []
        for m in range(MODES):
            d = c * MODES + m
            shifted.append(rows if d == 0 else pltpu.roll(rows, NC - d, 1))
        high, low = parts(jnp.concatenate(shifted, axis=0))
        cp_ref[c] = mul(high, pick) + mul(low, pick)

    pl.semaphore_wait(barrier, 22)

    def remote(src, dst, ssem, rsem, device):
        return pltpu.make_async_remote_copy(
            src_ref=src, dst_ref=dst, send_sem=ssem, recv_sem=rsem,
            device_id=device, device_id_type=MESH,
        )

    def neighbour(k, src, dst, d):
        return remote(src, dst, nb_ssem.at[k], nb_rsem.at[k], chain(d))

    left_copy = neighbour(0, left_out, left_in, -1)
    left_copy.start()
    right_copy = neighbour(1, right_out, right_in, 1)
    right_copy.start()
    colour = j % 4
    coarse_copies = []
    for k, d in enumerate((1, -1, -2)):
        coarse_copies.append(
            remote(cp_ref.at[core], crow_ref.at[0, colour], coarse_ssem.at[k], coarse_rsem.at[k], chain(d))
        )
    for k, d in enumerate((1, 0, -1, -2)):
        coarse_copies.append(
            remote(
                cp_ref.at[1 - core], crow_ref.at[1, colour], coarse_ssem.at[3 + k],
                coarse_rsem.at[3 + k], beside(d),
            )
        )

    for d in (2, 1, 3):
        pl.semaphore_signal(plane_sem, inc=1, device_id=peer(d, 0, 0), device_id_type=MESH)
    for copy in coarse_copies:
        copy.start()
    crow_ref[0, colour] = cp_ref[core]

    load.wait()

    def split_rows(i, c):
        rows = pl.ds(pl.multiple_of(i * 128, 128), 128)
        high, low = parts(schur_ref[rows, :])
        sh_ref[rows, :] = high
        sl_ref[rows, :] = low
        for ref, part in ((sh_ref, high), (sl_ref, low)):
            ref[rows, 0:M] = (-mul(part[:, :M], hot, NT)).astype(BF16)
        return c

    def split_columns(i, c):
        cols = pl.ds(pl.multiple_of(i * 128, 128), 128)
        for ref in (sh_ref, sl_ref):
            ref[0:M, cols] = (-mul(hot, ref[0:M, cols])).astype(BF16)
        return c

    lax.fori_loop(0, 6, split_rows, 0)
    pl.semaphore_wait(plane_sem, 3)
    for d in (2, 1, 3):
        pl.semaphore_signal(all_sem, inc=1, device_id=peer(0, d, 0), device_id_type=MESH)
    lax.fori_loop(0, 6, split_columns, 0)
    pl.semaphore_wait(all_sem, 3)

    def all_wait(ref, count, sem):
        w = ref.at[pl.ds(0, count)]
        pltpu.make_async_copy(w, w, sem).wait()

    landing = pl.ds(pl.multiple_of(2 * place, 2), 2)

    def start_send(r, dy, dx, dz):
        remote(out_ref.at[r], in_ref.at[r, landing], send.at[r], recv.at[r], peer(dy, dx, dz)).start()

    def send_own(r):
        in_ref[r, landing] = out_ref[r]

    def send_all(r):
        every_peer(functools.partial(start_send, r))
        send_own(r)

    send_all(0)

    first = j > 0
    last = j < CHAIN - 1

    def apply_product(before, own):
        lifted = jnp.concatenate([jnp.where(first, before, 0.0), own], axis=1)
        return mulw(lifted, sh_ref[...], sl_ref[...])

    def apply_send(i, values):
        fwd[i] = values
        copy = neighbour(3 + 2 * i, fwd.at[i], fwd_in.at[i], 1)
        copy.start()
        return copy

    def apply_middle(i, copy, values):
        copy.wait_recv()
        image = apply_product(fwd_in[i], values)
        back[i] = image[:, :M]
        copy_back = neighbour(4 + 2 * i, back.at[i], back_in.at[i], -1)
        copy_back.start()
        return copy_back, image[:, M:]

    def apply_end(i, copy_back, own):
        copy_back.wait_recv()
        return own + jnp.where(last, back_in[i], 0.0)

    left_copy.wait_recv()
    right_copy.wait_recv()
    following = jnp.where(last, left_in[...], 0.0)
    here = pl.ds(pl.multiple_of(colour * 8, 8), 8)
    after = pl.ds(pl.multiple_of(((j + 1) % 4) * 8, 8), 8)
    ahead = pl.ds(pl.multiple_of(((j + 3) % 4) * 8, 8), 8)
    xa_ref[...] = jnp.zeros((32, 768), F32)
    xa_ref[here, 0:M] = right_out[...]
    xa_ref[after, 0:M] = following
    xa_ref[here, M:] = left_out[...]
    xa_ref[ahead, M:] = right_in[...]
    wide_image = apply_product(xa_ref[:, M:], xa_ref[:, 0:M])
    wide_back[...] = wide_image[:, :M]
    wide_copy = neighbour(2, wide_back, wide_back_in, -1)
    wide_copy.start()
    xa_ref[:, M:] = wide_image[:, M:]

    pieces = []
    for block in (right_out[...], following):
        for m in range(MODES):
            pieces.append(jnp.broadcast_to(block[m : m + 1, :], (CASES, M)))
        pieces.append(jnp.zeros((32, M), F32))
    wh, wl = parts(jnp.transpose(jnp.concatenate(pieces, axis=0)))
    wh_ref[...] = wh
    wl_ref[...] = wl

    for copy in coarse_copies:
        copy.wait_recv()
    ch, cl = parts(crow_ref[...].reshape(384, 128))
    column = iota((128, 256), 1)
    spread = column // 2 + 4 * (column % 2)
    both = jnp.where(iota((128, 256), 0) == spread, 1.0, 0.0).astype(BF16)
    ch_ref[...] = mul(ch, both).astype(BF16)
    cl_ref[...] = mul(cl, both).astype(BF16)

    own_case = (iota((CASES, 256), 1) % CASES) == iota((CASES, 256), 0)
    slot = iota((MODES, 8, 128), 2) // CASES == iota((MODES, 8, 128), 0)

    def coefficients(r, field):
        product = mulw(field, wh_ref[...], wl_ref[...])
        flat = jnp.sum(jnp.where(own_case, product, 0.0), axis=0, keepdims=True)
        out_ref[r] = jnp.concatenate([flat[:, :128], flat[:, 128:]], axis=0)

    def picked(full, at):
        blocks = [
            jnp.sum(
                jnp.where(slot, full[at + c * 48 : at + (c + 1) * 48].reshape(MODES, 8, 128), 0.0),
                axis=0,
            )
            for c in range(4)
        ]
        return jnp.concatenate(blocks, axis=0)

    def coarse(r):
        all_wait(in_ref.at[r], 254, recv.at[r])
        gh, gl = parts(in_ref[r])
        both = mul(ch_ref[...], jnp.concatenate([gh, gl], axis=1))
        full = both[:, :128] + both[:, 128:] + mul(cl_ref[...], gh)
        pair_out[r] = picked(full, 192)
        copy = remote(pair_out.at[r], pair_in.at[r], pair_ssem.at[r], pair_rsem.at[r], beside(0))
        copy.start()
        mine = picked(full, 0)
        copy.wait_recv()
        turned = jnp.transpose(mine + pair_in[r])
        return jnp.sum(turned.reshape(8, CASES, 32), axis=0)

    def grams(a, blocks):
        spare = jnp.zeros((128 - CASES * len(blocks), M), F32)
        return mul3(a, jnp.concatenate([*blocks, spare], axis=0), NT)

    def gram_z(i, values):
        gz_out[i] = values
        for dz in (4, 3, 5, 2, 6, 1, 7):
            remote(gz_out.at[i], gz_in.at[i, z], gz_ssem.at[i], gz_rsem.at[i], peer(0, 0, dz)).start()
        gz_in[i, z] = values

    def gram_y(i):
        all_wait(gz_in.at[i], NZ - 1, gz_rsem.at[i])
        values = jnp.sum(gz_in[i], axis=0)
        gy_out[i] = values
        for dy, dx in FACES[:15]:
            remote(
                gy_out.at[i], gy_in.at[i, face], gy_ssem.at[i], gy_rsem.at[i], peer(dy, dx, 0)
            ).start()
        gy_in[i, face] = values

    def gram_pair(i):
        all_wait(gy_in.at[i], NY * NX - 1, gy_rsem.at[i])
        values = jnp.sum(gy_in[i], axis=0)
        gc_out[i] = values
        copy = remote(gc_out.at[i], gc_in.at[i], gc_ssem.at[i], gc_rsem.at[i], beside(0))
        copy.start()
        return copy, values

    def gram_end(i, copy, values):
        copy.wait_recv()
        return values + gc_in[i]

    right = right_ref[...]
    scale = scale_ref[...]
    y0 = coarse(0)
    wide_copy.wait_recv()
    xa_ref[:, M:] = xa_ref[:, M:] + jnp.where(last, wide_back_in[...], 0.0)
    moved = mul3(y0, xa_ref[...])
    mult = moved[:, :M]
    tt = right - moved[:, M:]

    coefficients(1, tt)
    send_all(1)
    resid = tt - mul3(coarse(1), xa_ref[:, 0:M])
    scaled = scale * resid

    coefficients(2, scaled)
    copy = apply_send(0, scaled)
    send_all(2)
    copy_back, own = apply_middle(0, copy, scaled)
    y2 = coarse(2)
    p = apply_end(0, copy_back, own)
    moved = mul3(y2, xa_ref[...])
    a = scaled - moved[:, :M]
    p = p - moved[:, M:]

    coefficients(3, p)
    send_all(3)
    gram_z(0, grams(a, (p, resid)))
    q = p - mul3(coarse(3), xa_ref[:, 0:M])
    scaled = scale * q

    coefficients(4, scaled)
    copy = apply_send(1, scaled)
    send_all(4)
    copy_back, own = apply_middle(1, copy, scaled)
    gram_y(0)
    crossed = grams(a, (q,))
    y4 = coarse(4)
    u = apply_end(1, copy_back, own)
    moved = mul3(y4, xa_ref[...])
    w = scaled - moved[:, :M]
    u = u - moved[:, M:]

    coefficients(5, u)
    lane = iota((CASES, 128), 1)
    gram_z(1, grams(w, (p, u, resid, q)) + jnp.where(lane >= 64, pltpu.roll(crossed, 64, 1), 0.0))
    far_peers(functools.partial(start_send, 5))
    copy, values = gram_pair(0)
    near_peers(functools.partial(start_send, 5))
    send_own(5)
    gram_y(1)
    sums = gram_end(0, copy, values)
    ap, ar = (sums[:, k * CASES : (k + 1) * CASES] for k in range(2))
    eye = jnp.where(iota((CASES, CASES), 0) == iota((CASES, CASES), 1), 1.0, 0.0)
    inverse = eliminate(ap, eye)
    alpha = exact(inverse, ar)
    v = u - mul3(coarse(5), xa_ref[:, 0:M])
    copy, values = gram_pair(1)
    sums = gram_end(1, copy, values)
    wp, wu, wr, wq, aq = (sums[:, k * CASES : (k + 1) * CASES] for k in range(5))
    across = exact(inverse, wp, NT)
    stepped = exact(jnp.concatenate([wq, aq], axis=0), alpha)
    rest = ar - stepped[CASES:]
    reduced = exact(across, rest, TN)
    gamma = eliminate(wu - exact(wp, across), wr - stepped[:CASES] - reduced)
    delta = alpha - exact(across, gamma)
    mix = jnp.transpose(jnp.concatenate([delta, gamma], axis=1))
    mixed = exact(mix[:CASES], jnp.concatenate([a, q], axis=1)) + exact(
        mix[CASES:], jnp.concatenate([w, v], axis=1)
    )
    mult_ref[...] = mult + mixed[:, :M]
    resid_ref[...] = resid - mixed[:, M:]

    left_copy.wait_send()
    right_copy.wait_send()
    for copy in coarse_copies:
        copy.wait_send()
    pltpu.make_async_copy(wide_back, wide_back, nb_ssem.at[2]).wait()
    for i in range(2):
        pltpu.make_async_copy(fwd.at[i], fwd.at[i], nb_ssem.at[3 + 2 * i]).wait()
        pltpu.make_async_copy(back.at[i], back.at[i], nb_ssem.at[4 + 2 * i]).wait()
        all_wait(gz_in.at[i], NZ - 1, gz_ssem.at[i])
        all_wait(gy_in.at[i], NY * NX - 1, gy_ssem.at[i])
        pltpu.make_async_copy(gc_out.at[i], gc_out.at[i], gc_ssem.at[i]).wait()
    for r in range(6):
        all_wait(in_ref.at[r], 254, send.at[r])
        pltpu.make_async_copy(pair_out.at[r], pair_out.at[r], pair_ssem.at[r]).wait()


def shards(right, schur, modes, count, order, scale, loads, coarse):
    vmem = pl.BlockSpec(memory_space=pltpu.VMEM)
    dma = pltpu.SemaphoreType.DMA
    regular = pltpu.SemaphoreType.REGULAR
    v = pltpu.VMEM
    mult, resid = pl.pallas_call(
        kernel,
        name="feti",
        out_shape=(jax.ShapeDtypeStruct((CASES, M), F32),) * 2,
        in_specs=[vmem, pl.BlockSpec(memory_space=pltpu.HBM)] + [vmem] * 6,
        out_specs=(vmem, vmem),
        scratch_shapes=[
            v((768, 768), F32), v((768, 768), BF16), v((768, 768), BF16),
            v((M, 256), BF16), v((M, 256), BF16), v((32, 768), F32),
            v((2, 48, 128), F32), v((2, 4, 48, 128), F32), v((384, 256), BF16), v((384, 256), BF16),
            v((6, 2, 128), F32), v((6, 256, 128), F32), v((6, 32, 128), F32), v((6, 32, 128), F32),
            v((2, 16, 128), F32), v((2, NZ, 16, 128), F32),
            v((2, 16, 128), F32), v((2, NY * NX, 16, 128), F32),
            v((2, 16, 128), F32), v((2, 16, 128), F32),
            v((8, M), F32), v((8, M), F32), v((8, M), F32), v((8, M), F32),
            v((2, 16, M), F32), v((2, 16, M), F32), v((32, M), F32), v((32, M), F32),
            v((2, 16, M), F32), v((2, 16, M), F32),
            v((8, 128), F32),
            dma, regular, regular, dma((7,)), dma((7,)), dma((6,)), dma((6,)), dma((6,)), dma((6,)),
            dma((2,)), dma((2,)), dma((2,)), dma((2,)), dma((2,)), dma((2,)), dma((7,)), dma((7,)),
        ],
        compiler_params=pltpu.CompilerParams(
            collective_id=0, has_side_effects=True, vmem_limit_bytes=60 * 1024 * 1024
        ),
    )(
        right.reshape(CASES, M), schur.reshape(768, 768), modes.reshape(MODES, 1, 768), count,
        order.reshape(1, M), scale.reshape(1, M), loads.reshape(MODES, 1, CASES), coarse,
    )
    return mult.reshape(1, 1, CASES, M), resid.reshape(1, 1, CASES, M)


def solution(mesh):
    field = P("sub", "cluster", None, None)
    return jax.shard_map(
        shards,
        mesh=mesh,
        in_specs=(
            field, field, field, P("sub", "cluster"), P("sub", "cluster", None),
            P("sub", "cluster", None), field, P(("cluster", "sub"), None),
        ),
        out_specs=(field, field),
        check_vma=False,
    )
```

time: 91.7 us -> 81.7 us (0.89)
  Pallas kernels: 83.2 us -> 77.4 us
  local copies, waits for them, and re-layouts: 6.67 us -> 2.69 us
    pallas_call x1, Pallas kernels: 83.2 us -> 77.4 us  [shards(): pl.pallas_call(kernel, name='feti', out_shape=(jax.ShapeDtypeStruct((CASE...]
    reshape x2 -> x0, local copies, waits for them, and re-layouts: 2.08 us -> none  [the longest x1 1.55 us: coarse_blocks(): c = rows.reshape(MODES, NY, NZ, NSUB, MODES)]
    pad x1 -> x0, local copies, waits for them, and re-layouts: 1.26 us -> none  [coarse_blocks(): both = jnp.pad(both, ((0, 0), (0, 2), (0, 0), (0, 0), (0, 0)))]
    unnamed x17 -> x2, local copies, waits for them, and re-layouts: 2.72 us -> 2.69 us
where the time goes in v1:
time: 81.7 us; the launch traced here: 81.4 us
  Pallas kernels  77.4 us (95%)
  local copies, waits for them, and re-layouts  2.69 us (3%)
  between operations  1.29 us (2%)
    pallas_call x1, Pallas kernels, shards(): pl.pallas_call(kernel, name='feti', out_shape=(jax.ShapeDtypeStruct((CASE...  77.4 us
    unnamed x2, local copies, waits for them, and re-layouts  2.69 us

profile of v1, /device:TPU:1, one launch (start us, length us, event | category | flops | bytes accessed | tf_op | source)
XLA Modules:
  0.0 81.4 jit_solution(15676209077254303916)
XLA Ops:
  1.3 77.4 %feti.1 = (f32[16,384]{1,0:T(8,128)}, f32[16,384]{1,0:T(8,128)}) custom-call(f32[16,384]{1,0:T(8,128)} %bitcast.9, f32[768,768]{1,0:T(8,128)} %bitcast.8, f32[6,1,768]{2,1,0:T(1,128)} %bitcast.12, s32[1,1]{1,0:T(1,128)S(6)} %copy.12.count_ref, s32[1,384]{1,0:T(1,128)} %bitcast.14, f32[1,384]{1,0:T(1,128)} %bitcast.15, f32[6,1,16]{2,1,0:T(1,128)} %bitcast.13, ...), custom_call_target="tpu_custom_call" | custom-call | tf_op jit(solution)/shard_map/feti/pallas_call | solution.py:490
  78.7 1.3 %copy.13 = f32[1,1,16,384]{3,2,1,0:T(8,128)} copy(f32[1,1,16,384]{3,2,1,0:T(8,128)} %bitcast.11) | data formatting | bytes 49152
  80.1 1.3 %copy.14 = f32[1,1,16,384]{3,2,1,0:T(8,128)} copy(f32[1,1,16,384]{3,2,1,0:T(8,128)} %bitcast.10) | data formatting | bytes 49152

commit v2 on v1

--- a/solution.py
+++ b/solution.py
@@ -84,15 +84,26 @@
     )
 
 
-FACES = (
-    (2, 2), (2, 1), (2, 3), (1, 2), (3, 2), (2, 0), (0, 2), (1, 1), (1, 3), (3, 1), (3, 3),
-    (0, 1), (0, 3), (1, 0), (3, 0), (0, 0),
+def ring(distance, size):
+    return min(distance, size - distance)
+
+
+OFFSETS = sorted(
+    (
+        (dy, dx, dz)
+        for dy in (2, 1, 3, 0)
+        for dx in (2, 1, 3, 0)
+        for dz in (4, 3, 5, 2, 6, 1, 7, 0)
+        if dy or dx or dz
+    ),
+    key=lambda o: -(ring(o[0], NY) + ring(o[1], NX) + ring(o[2], NZ)),
 )
 
 
 def kernel(
-    right_ref, schur_hbm, modes_ref, count_ref, order_ref, scale_ref, loads_ref, coarse_ref,
+    right_hbm, schur_hbm, modes_hbm, count_hbm, order_hbm, scale_hbm, loads_hbm, coarse_hbm,
     mult_ref, resid_ref,
+    right_ref, modes_ref, count_ref, order_ref, scale_ref, loads_ref, coarse_ref,
     schur_ref, sh_ref, sl_ref, wh_ref, wl_ref, xa_ref,
     cp_ref, crow_ref, ch_ref, cl_ref,
     out_ref, in_ref, pair_out, pair_in,
@@ -113,42 +124,18 @@
     place = j * NX + x
     face = y * NX + x
 
-    load = pltpu.make_async_copy(schur_hbm, schur_ref, load_sem)
-    load.start()
-
     def chain(d):
         return ((j + d + CHAIN) % CHAIN, s)
 
     def beside(d):
         return ((j + d + CHAIN) % CHAIN, other)
 
+    ys = [((y + d) % NY) * NZ for d in range(NY)]
+    zs = [(z + d) % NZ for d in range(NZ)]
+    xs = [((x + d) % NX) * 2 + core for d in range(NX)]
+
     def peer(dy, dx, dz):
-        return (((y + dy) % NY) * NZ + (z + dz) % NZ, ((x + dx) % NX) * 2 + core)
-
-    def z_offset(i):
-        half = (i + 1) // 2
-        return 4 + half * (1 - 2 * (i % 2))
-
-    def run(faces, low, high, act):
-        for dy, dx in faces:
-            def body(i, c, dy=dy, dx=dx):
-                act(dy, dx, z_offset(i))
-                return c
-
-            lax.fori_loop(low, high, body, 0)
-
-    def far_peers(act):
-        run(FACES[:11], 0, 5, act)
-        run(FACES[:5], 5, 8, act)
-
-    def near_peers(act):
-        run(FACES[11:], 0, 5, act)
-        run(FACES[5:15], 5, 8, act)
-        run(FACES[15:], 5, 7, act)
-
-    def every_peer(act):
-        far_peers(act)
-        near_peers(act)
+        return (ys[dy] + zs[dz], xs[dx])
 
     barrier = pltpu.get_barrier_semaphore()
 
@@ -164,6 +151,21 @@
         greet(peer(d, 0, 0))
         greet(peer(0, d, 0))
     greet(beside(0))
+
+    loads = [
+        pltpu.make_async_copy(src, dst, load_sem.at[k])
+        for k, (src, dst) in enumerate(
+            (
+                (loads_hbm, loads_ref), (count_hbm, count_ref), (modes_hbm, modes_ref),
+                (order_hbm, order_ref), (coarse_hbm, coarse_ref), (schur_hbm, schur_ref),
+                (right_hbm, right_ref), (scale_hbm, scale_ref),
+            )
+        )
+    ]
+    for copy in loads:
+        copy.start()
+    for copy in loads[:4]:
+        copy.wait()
 
     count = count_ref[...]
     active = jnp.where(iota((MODES, 1), 0) < count, 1.0, 0.0)
@@ -183,6 +185,7 @@
     left_out[...] = jnp.concatenate([permuted, jnp.zeros((2, M), F32)], axis=0)
     right_out[...] = jnp.concatenate([basis[:, M:], jnp.zeros((2, M), F32)], axis=0)
 
+    loads[4].wait()
     wanted = 12 * iota((NC, 128), 1)
     pick = jnp.where(iota((NC, 128), 0) == wanted, 1.0, 0.0).astype(BF16)
     rows = jnp.concatenate([coarse_ref[...], jnp.zeros((2, NC), F32)], axis=0)
@@ -229,7 +232,8 @@
         copy.start()
     crow_ref[0, colour] = cp_ref[core]
 
-    load.wait()
+    for copy in loads[5:]:
+        copy.wait()
 
     def split_rows(i, c):
         rows = pl.ds(pl.multiple_of(i * 128, 128), 128)
@@ -265,8 +269,12 @@
     def send_own(r):
         in_ref[r, landing] = out_ref[r]
 
+    def send_some(r, offsets):
+        for offset in offsets:
+            start_send(r, *offset)
+
     def send_all(r):
-        every_peer(functools.partial(start_send, r))
+        send_some(r, OFFSETS)
         send_own(r)
 
     send_all(0)
@@ -376,7 +384,9 @@
         all_wait(gz_in.at[i], NZ - 1, gz_rsem.at[i])
         values = jnp.sum(gz_in[i], axis=0)
         gy_out[i] = values
-        for dy, dx in FACES[:15]:
+        for dy, dx, dz in OFFSETS:
+            if dz:
+                continue
             remote(
                 gy_out.at[i], gy_in.at[i, face], gy_ssem.at[i], gy_rsem.at[i], peer(dy, dx, 0)
             ).start()
@@ -439,9 +449,9 @@
     coefficients(5, u)
     lane = iota((CASES, 128), 1)
     gram_z(1, grams(w, (p, u, resid, q)) + jnp.where(lane >= 64, pltpu.roll(crossed, 64, 1), 0.0))
-    far_peers(functools.partial(start_send, 5))
+    send_some(5, OFFSETS[:64])
     copy, values = gram_pair(0)
-    near_peers(functools.partial(start_send, 5))
+    send_some(5, OFFSETS[64:])
     send_own(5)
     gram_y(1)
     sums = gram_end(0, copy, values)
@@ -491,9 +501,11 @@
         kernel,
         name="feti",
         out_shape=(jax.ShapeDtypeStruct((CASES, M), F32),) * 2,
-        in_specs=[vmem, pl.BlockSpec(memory_space=pltpu.HBM)] + [vmem] * 6,
+        in_specs=[pl.BlockSpec(memory_space=pltpu.HBM)] * 8,
         out_specs=(vmem, vmem),
         scratch_shapes=[
+            v((CASES, M), F32), v((MODES, 1, 768), F32), v((1, 1), jnp.int32), v((1, M), jnp.int32),
+            v((1, M), F32), v((MODES, 1, CASES), F32), v((MODES, NC), F32),
             v((768, 768), F32), v((768, 768), BF16), v((768, 768), BF16),
             v((M, 256), BF16), v((M, 256), BF16), v((32, 768), F32),
             v((2, 48, 128), F32), v((2, 4, 48, 128), F32), v((384, 256), BF16), v((384, 256), BF16),
@@ -505,7 +517,7 @@
             v((2, 16, M), F32), v((2, 16, M), F32), v((32, M), F32), v((32, M), F32),
             v((2, 16, M), F32), v((2, 16, M), F32),
             v((8, 128), F32),
-            dma, regular, regular, dma((7,)), dma((7,)), dma((6,)), dma((6,)), dma((6,)), dma((6,)),
+            dma((8,)), regular, regular, dma((7,)), dma((7,)), dma((6,)), dma((6,)), dma((6,)), dma((6,)),
             dma((2,)), dma((2,)), dma((2,)), dma((2,)), dma((2,)), dma((2,)), dma((7,)), dma((7,)),
         ],
         compiler_params=pltpu.CompilerParams(

time: 81.7 us -> 79 us (0.967)
  Pallas kernels: 77.4 us -> 74.7 us
    pallas_call x1, Pallas kernels: 77.4 us -> 74.7 us  [shards(): pl.pallas_call(kernel, name='feti', out_shape=(jax.ShapeDtypeStruct((CASE...]
where the time goes in v2:
time: 79 us; the launch traced here: 78.7 us
  Pallas kernels  74.7 us (95%)
  local copies, waits for them, and re-layouts  2.69 us (3%)
  between operations  1.29 us (2%)
    pallas_call x1, Pallas kernels, shards(): pl.pallas_call(kernel, name='feti', out_shape=(jax.ShapeDtypeStruct((CASE...  74.7 us
    unnamed x2, local copies, waits for them, and re-layouts  2.69 us

profile of v2, /device:TPU:1, one launch (start us, length us, event | category | flops | bytes accessed | tf_op | source)
XLA Modules:
  0.0 78.7 jit_solution(9814221792356226449)
XLA Ops:
  1.3 74.7 %feti.1 = (f32[16,384]{1,0:T(8,128)}, f32[16,384]{1,0:T(8,128)}) custom-call(f32[16,384]{1,0:T(8,128)} %bitcast.9, f32[768,768]{1,0:T(8,128)} %bitcast.8, f32[6,1,768]{2,1,0:T(1,128)} %bitcast.12, s32[1,1]{1,0:T(1,128)S(6)} %copy.12.count_hbm, s32[1,384]{1,0:T(1,128)} %bitcast.14, f32[1,384]{1,0:T(1,128)} %bitcast.15, f32[6,1,16]{2,1,0:T(1,128)} %bitcast.13, ...), custom_call_target="tpu_custom_call" | custom-call | tf_op jit(solution)/shard_map/feti/pallas_call | solution.py:500
  76.0 1.3 %copy.13 = f32[1,1,16,384]{3,2,1,0:T(8,128)} copy(f32[1,1,16,384]{3,2,1,0:T(8,128)} %bitcast.11) | data formatting | bytes 49152
  77.4 1.3 %copy.14 = f32[1,1,16,384]{3,2,1,0:T(8,128)} copy(f32[1,1,16,384]{3,2,1,0:T(8,128)} %bitcast.10) | data formatting | bytes 49152

commit v3 on v2

--- a/solution.py
+++ b/solution.py
@@ -100,9 +100,12 @@
 )
 
 
+FACES = tuple((dy, dx) for dy, dx, dz in OFFSETS if not dz)
+
+
 def kernel(
     right_hbm, schur_hbm, modes_hbm, count_hbm, order_hbm, scale_hbm, loads_hbm, coarse_hbm,
-    mult_ref, resid_ref,
+    both_ref,
     right_ref, modes_ref, count_ref, order_ref, scale_ref, loads_ref, coarse_ref,
     schur_ref, sh_ref, sl_ref, wh_ref, wl_ref, xa_ref,
     cp_ref, crow_ref, ch_ref, cl_ref,
@@ -110,8 +113,8 @@
     gz_out, gz_in, gy_out, gy_in, gc_out, gc_in,
     left_out, left_in, right_out, right_in,
     fwd, fwd_in, wide_back, wide_back_in, back, back_in,
-    tmp_ref,
-    load_sem, plane_sem, all_sem, coarse_ssem, coarse_rsem, send, recv, pair_ssem, pair_rsem,
+    tmp_ref, line_ref,
+    load_sem, line_sems, coarse_ssem, coarse_rsem, send, recv, pair_ssem, pair_rsem,
     gz_ssem, gz_rsem, gy_ssem, gy_rsem, gc_ssem, gc_rsem, nb_ssem, nb_rsem,
 ):
     j = lax.axis_index("cluster")
@@ -121,8 +124,8 @@
     x = s // 2
     core = s % 2
     other = s + 1 - 2 * core
-    place = j * NX + x
     face = y * NX + x
+    place = face * NZ + z
 
     def chain(d):
         return ((j + d + CHAIN) % CHAIN, s)
@@ -147,9 +150,8 @@
     for d in (-2, 2, -1, 1):
         greet(chain(d))
         greet(beside(d))
-    for d in (2, 1, 3):
-        greet(peer(d, 0, 0))
-        greet(peer(0, d, 0))
+    for dy, dx in FACES:
+        greet(peer(dy, dx, 0))
     greet(beside(0))
 
     loads = [
@@ -186,7 +188,8 @@
     right_out[...] = jnp.concatenate([basis[:, M:], jnp.zeros((2, M), F32)], axis=0)
 
     loads[4].wait()
-    wanted = 12 * iota((NC, 128), 1)
+    chip = iota((NC, 128), 1)
+    wanted = (chip // 32) * 384 + (chip % NZ) * 48 + (chip // NZ % NX) * 12
     pick = jnp.where(iota((NC, 128), 0) == wanted, 1.0, 0.0).astype(BF16)
     rows = jnp.concatenate([coarse_ref[...], jnp.zeros((2, NC), F32)], axis=0)
     for c in range(2):
@@ -197,7 +200,7 @@
         high, low = parts(jnp.concatenate(shifted, axis=0))
         cp_ref[c] = mul(high, pick) + mul(low, pick)
 
-    pl.semaphore_wait(barrier, 22)
+    pl.semaphore_wait(barrier, 31)
 
     def remote(src, dst, ssem, rsem, device):
         return pltpu.make_async_remote_copy(
@@ -207,6 +210,15 @@
 
     def neighbour(k, src, dst, d):
         return remote(src, dst, nb_ssem.at[k], nb_rsem.at[k], chain(d))
+
+    def all_wait(ref, count, sem):
+        w = ref.at[pl.ds(0, count)]
+        pltpu.make_async_copy(w, w, sem).wait()
+
+    line = pl.ds(pl.multiple_of(2 * z, 2), 2)
+    for dz in (4, 3, 5, 2, 6, 1, 7):
+        remote(out_ref.at[0], line_ref.at[line], line_sems.at[0], line_sems.at[1], peer(0, 0, dz)).start()
+    line_ref[line] = out_ref[0]
 
     left_copy = neighbour(0, left_out, left_in, -1)
     left_copy.start()
@@ -226,8 +238,6 @@
             )
         )
 
-    for d in (2, 1, 3):
-        pl.semaphore_signal(plane_sem, inc=1, device_id=peer(d, 0, 0), device_id_type=MESH)
     for copy in coarse_copies:
         copy.start()
     crow_ref[0, colour] = cp_ref[core]
@@ -251,15 +261,12 @@
         return c
 
     lax.fori_loop(0, 6, split_rows, 0)
-    pl.semaphore_wait(plane_sem, 3)
-    for d in (2, 1, 3):
-        pl.semaphore_signal(all_sem, inc=1, device_id=peer(0, d, 0), device_id_type=MESH)
+    all_wait(line_ref, 14, line_sems.at[1])
+    block = pl.ds(pl.multiple_of(16 * face, 16), 16)
+    for dy, dx in FACES:
+        remote(line_ref, in_ref.at[0, block], send.at[0], recv.at[0], peer(dy, dx, 0)).start()
+    in_ref[0, block] = line_ref[...]
     lax.fori_loop(0, 6, split_columns, 0)
-    pl.semaphore_wait(all_sem, 3)
-
-    def all_wait(ref, count, sem):
-        w = ref.at[pl.ds(0, count)]
-        pltpu.make_async_copy(w, w, sem).wait()
 
     landing = pl.ds(pl.multiple_of(2 * place, 2), 2)
 
@@ -277,7 +284,6 @@
         send_some(r, OFFSETS)
         send_own(r)
 
-    send_all(0)
 
     first = j > 0
     last = j < CHAIN - 1
@@ -334,7 +340,8 @@
         copy.wait_recv()
     ch, cl = parts(crow_ref[...].reshape(384, 128))
     column = iota((128, 256), 1)
-    spread = column // 2 + 4 * (column % 2)
+    chip = column // 2
+    spread = chip + (column % 2) * jnp.where(chip % NZ == NZ - 1, 25, 1)
     both = jnp.where(iota((128, 256), 0) == spread, 1.0, 0.0).astype(BF16)
     ch_ref[...] = mul(ch, both).astype(BF16)
     cl_ref[...] = mul(cl, both).astype(BF16)
@@ -358,7 +365,7 @@
         return jnp.concatenate(blocks, axis=0)
 
     def coarse(r):
-        all_wait(in_ref.at[r], 254, recv.at[r])
+        all_wait(in_ref.at[r], 254 if r else 240, recv.at[r])
         gh, gl = parts(in_ref[r])
         both = mul(ch_ref[...], jnp.concatenate([gh, gl], axis=1))
         full = both[:, :128] + both[:, 128:] + mul(cl_ref[...], gh)
@@ -384,9 +391,7 @@
         all_wait(gz_in.at[i], NZ - 1, gz_rsem.at[i])
         values = jnp.sum(gz_in[i], axis=0)
         gy_out[i] = values
-        for dy, dx, dz in OFFSETS:
-            if dz:
-                continue
+        for dy, dx in FACES:
             remote(
                 gy_out.at[i], gy_in.at[i, face], gy_ssem.at[i], gy_rsem.at[i], peer(dy, dx, 0)
             ).start()
@@ -430,54 +435,52 @@
 
     coefficients(3, p)
     send_all(3)
-    gram_z(0, grams(a, (p, resid)))
     q = p - mul3(coarse(3), xa_ref[:, 0:M])
     scaled = scale * q
 
     coefficients(4, scaled)
     copy = apply_send(1, scaled)
     send_all(4)
+    gram_z(0, grams(a, (p, resid, q)))
     copy_back, own = apply_middle(1, copy, scaled)
-    gram_y(0)
-    crossed = grams(a, (q,))
     y4 = coarse(4)
     u = apply_end(1, copy_back, own)
     moved = mul3(y4, xa_ref[...])
     w = scaled - moved[:, :M]
     u = u - moved[:, M:]
 
+    gram_z(1, grams(w, (p, u, resid, q)))
     coefficients(5, u)
-    lane = iota((CASES, 128), 1)
-    gram_z(1, grams(w, (p, u, resid, q)) + jnp.where(lane >= 64, pltpu.roll(crossed, 64, 1), 0.0))
-    send_some(5, OFFSETS[:64])
+    send_some(5, OFFSETS[:48])
+    gram_y(0)
+    send_some(5, OFFSETS[48:100])
+    gram_y(1)
+    send_some(5, OFFSETS[100:])
+    send_own(5)
     copy, values = gram_pair(0)
-    send_some(5, OFFSETS[64:])
-    send_own(5)
-    gram_y(1)
     sums = gram_end(0, copy, values)
-    ap, ar = (sums[:, k * CASES : (k + 1) * CASES] for k in range(2))
+    ap, ar, aq = (sums[:, k * CASES : (k + 1) * CASES] for k in range(3))
     eye = jnp.where(iota((CASES, CASES), 0) == iota((CASES, CASES), 1), 1.0, 0.0)
     inverse = eliminate(ap, eye)
     alpha = exact(inverse, ar)
+    rest = ar - exact(aq, alpha)
     v = u - mul3(coarse(5), xa_ref[:, 0:M])
+    aq_fields = jnp.concatenate([a, q], axis=1)
+    first_step = exact(alpha, aq_fields, TN)
     copy, values = gram_pair(1)
     sums = gram_end(1, copy, values)
-    wp, wu, wr, wq, aq = (sums[:, k * CASES : (k + 1) * CASES] for k in range(5))
+    wp, wu, wr, wq = (sums[:, k * CASES : (k + 1) * CASES] for k in range(4))
     across = exact(inverse, wp, NT)
-    stepped = exact(jnp.concatenate([wq, aq], axis=0), alpha)
-    rest = ar - stepped[CASES:]
-    reduced = exact(across, rest, TN)
-    gamma = eliminate(wu - exact(wp, across), wr - stepped[:CASES] - reduced)
-    delta = alpha - exact(across, gamma)
-    mix = jnp.transpose(jnp.concatenate([delta, gamma], axis=1))
-    mixed = exact(mix[:CASES], jnp.concatenate([a, q], axis=1)) + exact(
-        mix[CASES:], jnp.concatenate([w, v], axis=1)
-    )
-    mult_ref[...] = mult + mixed[:, :M]
-    resid_ref[...] = resid - mixed[:, M:]
+    right_side = wr - exact(wq, alpha) - exact(across, rest, TN)
+    gamma = eliminate(wu - exact(wp, across), right_side)
+    turned = jnp.concatenate([w, v], axis=1) - exact(across, aq_fields, TN)
+    mixed = first_step + exact(gamma, turned, TN)
+    both_ref[0:CASES] = mult + mixed[:, :M]
+    both_ref[CASES:] = resid - mixed[:, M:]
 
     left_copy.wait_send()
     right_copy.wait_send()
+    all_wait(line_ref, 14, line_sems.at[0])
     for copy in coarse_copies:
         copy.wait_send()
     pltpu.make_async_copy(wide_back, wide_back, nb_ssem.at[2]).wait()
@@ -488,21 +491,20 @@
         all_wait(gy_in.at[i], NY * NX - 1, gy_ssem.at[i])
         pltpu.make_async_copy(gc_out.at[i], gc_out.at[i], gc_ssem.at[i]).wait()
     for r in range(6):
-        all_wait(in_ref.at[r], 254, send.at[r])
+        all_wait(in_ref.at[r], 254 if r else 240, send.at[r])
         pltpu.make_async_copy(pair_out.at[r], pair_out.at[r], pair_ssem.at[r]).wait()
 
 
 def shards(right, schur, modes, count, order, scale, loads, coarse):
     vmem = pl.BlockSpec(memory_space=pltpu.VMEM)
     dma = pltpu.SemaphoreType.DMA
-    regular = pltpu.SemaphoreType.REGULAR
     v = pltpu.VMEM
-    mult, resid = pl.pallas_call(
+    both = pl.pallas_call(
         kernel,
         name="feti",
-        out_shape=(jax.ShapeDtypeStruct((CASES, M), F32),) * 2,
+        out_shape=jax.ShapeDtypeStruct((2 * CASES, M), F32),
         in_specs=[pl.BlockSpec(memory_space=pltpu.HBM)] * 8,
-        out_specs=(vmem, vmem),
+        out_specs=vmem,
         scratch_shapes=[
             v((CASES, M), F32), v((MODES, 1, 768), F32), v((1, 1), jnp.int32), v((1, M), jnp.int32),
             v((1, M), F32), v((MODES, 1, CASES), F32), v((MODES, NC), F32),
@@ -516,8 +518,8 @@
             v((8, M), F32), v((8, M), F32), v((8, M), F32), v((8, M), F32),
             v((2, 16, M), F32), v((2, 16, M), F32), v((32, M), F32), v((32, M), F32),
             v((2, 16, M), F32), v((2, 16, M), F32),
-            v((8, 128), F32),
-            dma((8,)), regular, regular, dma((7,)), dma((7,)), dma((6,)), dma((6,)), dma((6,)), dma((6,)),
+            v((8, 128), F32), v((16, 128), F32),
+            dma((8,)), dma((2,)), dma((7,)), dma((7,)), dma((6,)), dma((6,)), dma((6,)), dma((6,)),
             dma((2,)), dma((2,)), dma((2,)), dma((2,)), dma((2,)), dma((2,)), dma((7,)), dma((7,)),
         ],
         compiler_params=pltpu.CompilerParams(
@@ -527,7 +529,7 @@
         right.reshape(CASES, M), schur.reshape(768, 768), modes.reshape(MODES, 1, 768), count,
         order.reshape(1, M), scale.reshape(1, M), loads.reshape(MODES, 1, CASES), coarse,
     )
-    return mult.reshape(1, 1, CASES, M), resid.reshape(1, 1, CASES, M)
+    return both[:CASES].reshape(1, 1, CASES, M), both[CASES:].reshape(1, 1, CASES, M)
 
 
 def solution(mesh):

time: 79 us -> 77.3 us (0.978)
  local copies, waits for them, and re-layouts: 2.69 us -> 1.38 us
    unnamed x2 -> x0, local copies, waits for them, and re-layouts: 2.69 us -> none
    reshape x0 -> x1, local copies, waits for them, and re-layouts: none -> 1.38 us  [shards(): both[CASES:].reshape(1, 1, CASES, M)]
where the time goes in v3:
time: 77.3 us; the launch traced here: 77.1 us
  Pallas kernels  74.4 us (96%)
  local copies, waits for them, and re-layouts  1.38 us (2%)
  between operations  1.29 us (2%)
    pallas_call x1, Pallas kernels, shards(): pl.pallas_call(kernel, name='feti', out_shape=jax.ShapeDtypeStruct((2 * C...  74.4 us

profile of v3, /device:TPU:1, one launch (start us, length us, event | category | flops | bytes accessed | tf_op | source)
XLA Modules:
  0.0 77.1 jit_solution(15655406254387958520)
XLA Ops:
  1.3 74.4 %feti.1 = f32[32,384]{1,0:T(8,128)} custom-call(f32[16,384]{1,0:T(8,128)} %bitcast.11, f32[768,768]{1,0:T(8,128)} %bitcast.10, f32[6,1,768]{2,1,0:T(1,128)} %bitcast.12, s32[1,1]{1,0:T(1,128)S(6)} %copy.10.count_hbm, s32[1,384]{1,0:T(1,128)} %bitcast.14, f32[1,384]{1,0:T(1,128)} %bitcast.15, f32[6,1,16]{2,1,0:T(1,128)} %bitcast.13, f32[6,1536]{1,0:T(8,128)} %coarse_hbm.1), custom_call_target="tpu_custom_call" | custom-call | tf_op jit(solution)/shard_map/feti/pallas_call | solution.py:502
  75.7 1.4 %slice_bitcast_fusion = (f32[1,1,16,384]{3,2,1,0:T(8,128)}, f32[1,1,16,384]{3,2,1,0:T(8,128)}) fusion(f32[32,384]{1,0:T(8,128)} %feti.1), kind=kLoop, calls=%fused_computation | loop fusion | bytes 98304 | tf_op jit(solution)/shard_map/reshape | solution.py:532

commit v4 on v3

--- a/solution.py
+++ b/solution.py
@@ -414,13 +414,14 @@
     y0 = coarse(0)
     wide_copy.wait_recv()
     xa_ref[:, M:] = xa_ref[:, M:] + jnp.where(last, wide_back_in[...], 0.0)
-    moved = mul3(y0, xa_ref[...])
+    xh, xl = parts(xa_ref[...])
+    moved = mulw(y0, xh, xl)
     mult = moved[:, :M]
     tt = right - moved[:, M:]
 
     coefficients(1, tt)
     send_all(1)
-    resid = tt - mul3(coarse(1), xa_ref[:, 0:M])
+    resid = tt - mulw(coarse(1), xh[:, :M], xl[:, :M])
     scaled = scale * resid
 
     coefficients(2, scaled)
@@ -429,23 +430,23 @@
     copy_back, own = apply_middle(0, copy, scaled)
     y2 = coarse(2)
     p = apply_end(0, copy_back, own)
-    moved = mul3(y2, xa_ref[...])
+    moved = mulw(y2, xh, xl)
     a = scaled - moved[:, :M]
     p = p - moved[:, M:]
 
     coefficients(3, p)
     send_all(3)
-    q = p - mul3(coarse(3), xa_ref[:, 0:M])
+    q = p - mulw(coarse(3), xh[:, :M], xl[:, :M])
     scaled = scale * q
 
     coefficients(4, scaled)
     copy = apply_send(1, scaled)
     send_all(4)
+    copy_back, own = apply_middle(1, copy, scaled)
     gram_z(0, grams(a, (p, resid, q)))
-    copy_back, own = apply_middle(1, copy, scaled)
     y4 = coarse(4)
     u = apply_end(1, copy_back, own)
-    moved = mul3(y4, xa_ref[...])
+    moved = mulw(y4, xh, xl)
     w = scaled - moved[:, :M]
     u = u - moved[:, M:]
 
@@ -464,7 +465,7 @@
     inverse = eliminate(ap, eye)
     alpha = exact(inverse, ar)
     rest = ar - exact(aq, alpha)
-    v = u - mul3(coarse(5), xa_ref[:, 0:M])
+    v = u - mulw(coarse(5), xh[:, :M], xl[:, :M])
     aq_fields = jnp.concatenate([a, q], axis=1)
     first_step = exact(alpha, aq_fields, TN)
     copy, values = gram_pair(1)

time: 77.3 us -> 77.2 us (level)
  no operation moved by 1% of the time
where the time goes in v4:
time: 77.2 us; the launch traced here: 77.1 us
  Pallas kernels  74.4 us (96%)
  local copies, waits for them, and re-layouts  1.38 us (2%)
  between operations  1.29 us (2%)
    pallas_call x1, Pallas kernels, shards(): pl.pallas_call(kernel, name='feti', out_shape=jax.ShapeDtypeStruct((2 * C...  74.4 us

profile of v4, /device:TPU:1, one launch (start us, length us, event | category | flops | bytes accessed | tf_op | source)
XLA Modules:
  0.0 77.1 jit_solution(12705040145736430815)
XLA Ops:
  1.3 74.4 %feti.1 = f32[32,384]{1,0:T(8,128)} custom-call(f32[16,384]{1,0:T(8,128)} %bitcast.11, f32[768,768]{1,0:T(8,128)} %bitcast.10, f32[6,1,768]{2,1,0:T(1,128)} %bitcast.12, s32[1,1]{1,0:T(1,128)S(6)} %copy.10.count_hbm, s32[1,384]{1,0:T(1,128)} %bitcast.14, f32[1,384]{1,0:T(1,128)} %bitcast.15, f32[6,1,16]{2,1,0:T(1,128)} %bitcast.13, f32[6,1536]{1,0:T(8,128)} %coarse_hbm.1), custom_call_target="tpu_custom_call" | custom-call | tf_op jit(solution)/shard_map/feti/pallas_call | solution.py:503
  75.7 1.4 %slice_bitcast_fusion = (f32[1,1,16,384]{3,2,1,0:T(8,128)}, f32[1,1,16,384]{3,2,1,0:T(8,128)}) fusion(f32[32,384]{1,0:T(8,128)} %feti.1), kind=kLoop, calls=%fused_computation | loop fusion | bytes 98304 | tf_op jit(solution)/shard_map/reshape | solution.py:533

commit v5 on v3

--- a/solution.py
+++ b/solution.py
@@ -61,20 +61,24 @@
     shape = (CASES, 2 * CASES)
     row = iota(shape, 0)
     tile = jnp.concatenate([matrix, right], axis=1)
-    for k in range(0, CASES, 2):
-        c1 = jnp.broadcast_to(tile[:, k : k + 1], shape)
-        c2 = jnp.broadcast_to(tile[:, k + 1 : k + 2], shape)
-        r1 = jnp.broadcast_to(tile[k : k + 1, :], shape)
-        r2 = jnp.broadcast_to(tile[k + 1 : k + 2, :], shape)
-        p11 = jnp.broadcast_to(c1[k : k + 1, :], shape)
-        p21 = jnp.broadcast_to(c1[k + 1 : k + 2, :], shape)
-        p12 = jnp.broadcast_to(c2[k : k + 1, :], shape)
-        p22 = jnp.broadcast_to(c2[k + 1 : k + 2, :], shape)
-        factor = p21 / p11
-        s2 = (r2 - factor * r1) / (p22 - factor * p12)
-        s1 = (r1 - p12 * s2) / p11
-        rest = tile - c1 * s1 - c2 * s2
-        tile = jnp.where(row == k, s1, jnp.where(row == k + 1, s2, rest))
+    for k in range(0, CASES, 4):
+        c = [jnp.broadcast_to(tile[:, k + i : k + i + 1], shape) for i in range(4)]
+        r = [jnp.broadcast_to(tile[k + i : k + i + 1, :], shape) for i in range(4)]
+        p = [[jnp.broadcast_to(c[n][k + i : k + i + 1, :], shape) for n in range(4)] for i in range(4)]
+        for i in range(4):
+            factor = 1.0 / p[i][i]
+            r[i] = r[i] * factor
+            for n in range(i + 1, 4):
+                p[i][n] = p[i][n] * factor
+            for o in range(4):
+                if o != i:
+                    r[o] = r[o] - p[o][i] * r[i]
+                    for n in range(i + 1, 4):
+                        p[o][n] = p[o][n] - p[o][i] * p[i][n]
+        rest = tile - (c[0] * r[0] + c[1] * r[1]) - (c[2] * r[2] + c[3] * r[3])
+        for i in range(4):
+            rest = jnp.where(row == k + i, r[i], rest)
+        tile = rest
     return tile[:, CASES:]
 
 

time: 77.3 us -> 76.8 us (level)
  no operation moved by 1% of the time
where the time goes in v5:
time: 76.8 us; the launch traced here: 76.6 us
  Pallas kernels  74 us (96%)
  local copies, waits for them, and re-layouts  1.38 us (2%)
  between operations  1.29 us (2%)
    pallas_call x1, Pallas kernels, shards(): pl.pallas_call(kernel, name='feti', out_shape=jax.ShapeDtypeStruct((2 * C...  74 us

profile of v5, /device:TPU:1, one launch (start us, length us, event | category | flops | bytes accessed | tf_op | source)
XLA Modules:
  0.0 76.6 jit_solution(12316349652557462084)
XLA Ops:
  1.3 74.0 %feti.1 = f32[32,384]{1,0:T(8,128)} custom-call(f32[16,384]{1,0:T(8,128)} %bitcast.11, f32[768,768]{1,0:T(8,128)} %bitcast.10, f32[6,1,768]{2,1,0:T(1,128)} %bitcast.12, s32[1,1]{1,0:T(1,128)S(6)} %copy.10.count_hbm, s32[1,384]{1,0:T(1,128)} %bitcast.14, f32[1,384]{1,0:T(1,128)} %bitcast.15, f32[6,1,16]{2,1,0:T(1,128)} %bitcast.13, f32[6,1536]{1,0:T(8,128)} %coarse_hbm.1), custom_call_target="tpu_custom_call" | custom-call | tf_op jit(solution)/shard_map/feti/pallas_call | solution.py:506
  75.3 1.4 %slice_bitcast_fusion = (f32[1,1,16,384]{3,2,1,0:T(8,128)}, f32[1,1,16,384]{3,2,1,0:T(8,128)}) fusion(f32[32,384]{1,0:T(8,128)} %feti.1), kind=kLoop, calls=%fused_computation | loop fusion | bytes 98304 | tf_op jit(solution)/shard_map/reshape | solution.py:536
